TPU v7x, 128 devices: a whole 4x4x4 slice. The times are simulated.
128 devices in a mesh: rollout: 16 (over y, x), section: 4 (over z), tensor: 2 (over core).
Axes of the slice: x: 4, y: 4, z: 4, core: 2. Of those that a mesh axis runs over, the one named last changes fastest.
Arguments:
- entering: bfloat16 [4, 512, 8192], P('section', 'tensor', 'rollout')
- arriving: bfloat16 [2, 512, 8192], P(None, 'tensor', 'rollout')
- w_query: bfloat16 [4, 8192, 4096], P('section', 'rollout', 'tensor'), may hold values from -0.0625 to 0.0625
- w_keyval: bfloat16 [4, 8192, 2, 1024], P('section', 'rollout', None, 'tensor'), may hold values from -0.0625 to 0.0625
- w_out: bfloat16 [4, 4096, 8192], P('section', 'tensor', 'rollout'), may hold values from -0.75 to 0.75
- query_bias: bfloat16 [4, 4096], P('section', 'tensor')
- keyval_bias: bfloat16 [4, 2, 1024], P('section', None, 'tensor'), may hold values from -3 to 3
- norm_gain: bfloat16 [4, 8192], P('section', 'rollout'), may hold values from 0.5 to 1.5
- resident_kv: bfloat16 [16, 4, 1120, 2, 1024], P('rollout', 'section', None, None, 'tensor')
- resumed_pages: int32 [16], replicated, may hold values from 24 to 32, as said below
- section_active: int32 [4], replicated, may hold values from 0 to 1, as said below
- block_table: int32 [16, 4, 38, 2], replicated, may hold values from 0 to 63, as said below
Outputs:
- section_out: bfloat16 [4, 3, 512, 8192], P('section', None, 'tensor', 'rollout')
- page_pool: bfloat16 [16, 4, 38, 32, 2, 1024], P('rollout', 'section', None, None, None, 'tensor')
Inputs may be any that keep to these rules, and one draw needn't show every extreme that they name: `resumed_pages`: some rollout has exactly 32 pages. `section_active`: exactly 3 sections hold a layer. `block_table`: entry [..., 0] names a decode device (rollout index times 4 plus section index) and entry [..., 1] a slot there; every pair of device and slot is named by exactly one page; the 38 pages of each rollout and section name any one decode device at most 1 times, and each of them reaches that bound for some device.
All inputs are finite; a program needn't handle non-finite values.
Results may differ from a plain program's by a relative error of at most 0.029.
Values may be sent and summed in bfloat16 or wider, within the bound.
No kernel may reach another device: no remote copies, remote signals or barrier semaphores. Data moves between devices by JAX's collectives and lax.ppermute only.
A program may use at most 128 MiB of HBM per device.

v0:
```python
import math

import jax
import jax.numpy as jnp
from jax import lax
from jax.sharding import PartitionSpec as P

D = 8192
HD = 128
BLOCK = 32
BLOCKS = 3
PAGE = 32


def from_behind(block, axis, distance):
    devices = range(lax.axis_size(axis))
    route = [(i - distance, i) for i in devices if i - distance in devices]
    return lax.ppermute(block, axis, route)


def rotary(values, positions):
    half = HD // 2
    freq = jnp.power(jnp.float32(1000000.0), -(jnp.arange(half, dtype=jnp.float32) * (2.0 / HD)))
    angle = positions.astype(jnp.float32)[:, None] * freq[None, :]
    cosine = jnp.cos(angle)[:, None, :]
    sine = jnp.sin(angle)[:, None, :]
    first = values[..., :half]
    second = values[..., half:]
    return jnp.concatenate(
        [first * cosine - second * sine, second * cosine + first * sine], axis=-1
    )


def attend(query, cache_keys, cache_vals, new_keys, new_vals, length, step):
    row_count, heads, width = query.shape
    kv_heads = cache_keys.shape[1]
    grouped = query.reshape(row_count, kv_heads, heads // kv_heads, width)
    scale = 1.0 / math.sqrt(width)
    cached = (
        jnp.einsum("tkgd,jkd->kgtj", grouped, cache_keys, preferred_element_type=jnp.float32)
        * scale
    )
    recent = (
        jnp.einsum("tkgd,jkd->kgtj", grouped, new_keys, preferred_element_type=jnp.float32) * scale
    )
    cache_seen = jnp.arange(cache_keys.shape[0], dtype=jnp.int32) < length
    recent_seen = (
        jnp.arange(new_keys.shape[0])[None, :] <= step * row_count + jnp.arange(row_count)[:, None]
    )
    cached = jnp.where(cache_seen, cached, -1e30)
    recent = jnp.where(recent_seen, recent, -1e30)
    scores = jnp.concatenate([cached, recent], axis=-1)
    peak = jnp.max(scores, axis=-1, keepdims=True)
    powers = jnp.exp(scores - peak)
    weights = (powers / jnp.sum(powers, axis=-1, keepdims=True)).astype(jnp.bfloat16)
    values = jnp.concatenate([cache_vals, new_vals], axis=0)
    mixed = jnp.einsum("kgtj,jkd->tkgd", weights, values, preferred_element_type=jnp.float32)
    return mixed.reshape(row_count, heads * width).astype(jnp.bfloat16)


def local(
    entering,
    arriving,
    w_query,
    w_keyval,
    w_out,
    query_bias,
    keyval_bias,
    norm_gain,
    resident_kv,
    resumed_pages,
    section_active,
    block_table,
):
    roll_count = lax.axis_size("rollout")
    section_count = lax.axis_size("section")
    tensor_count = lax.axis_size("tensor")
    rollout = lax.axis_index("rollout")
    section = lax.axis_index("section")
    tensor = lax.axis_index("tensor")
    width_block = w_query.shape[1]
    query_width = w_query.shape[2]
    kv_width = w_keyval.shape[3]
    kv_heads = kv_width // HD
    token_rows = entering.shape[1]
    block_rows = token_rows * tensor_count // roll_count
    weight_cat = jnp.concatenate(
        [w_query[0], w_keyval[0].reshape(width_block, 2 * kv_width)], axis=1
    )
    out_block = w_out[0]
    gain_block = norm_gain[0].astype(jnp.float32)
    query_shift = query_bias[0].astype(jnp.float32)
    key_shift = keyval_bias[0, 0].astype(jnp.float32)
    value_shift = keyval_bias[0, 1].astype(jnp.float32)
    active = section_active[section].astype(jnp.float32)
    length = resumed_pages[rollout] * PAGE + (section_count - 1 - section) * BLOCK
    resident = resident_kv[0, 0]
    context = resident.shape[0]
    cache_keys = resident[:, 0].reshape(context, kv_heads, HD)
    cache_vals = resident[:, 1].reshape(context, kv_heads, HD)
    fresh_keys = []
    fresh_vals = []

    def layer_core(normed_all, step):
        projected = lax.psum_scatter(
            jnp.dot(normed_all, weight_cat, preferred_element_type=jnp.float32).astype(
                jnp.bfloat16
            ),
            "rollout",
            scatter_dimension=0,
            tiled=True,
        ).astype(jnp.float32)
        positions = length + step * BLOCK + jnp.arange(block_rows, dtype=jnp.int32)
        query = rotary(
            (projected[:, :query_width] + query_shift).reshape(block_rows, query_width // HD, HD),
            positions,
        ).astype(jnp.bfloat16)
        new_key = rotary(
            (projected[:, query_width : query_width + kv_width] + key_shift).reshape(
                block_rows, kv_heads, HD
            ),
            positions,
        ).astype(jnp.bfloat16)
        new_value = (
            (projected[:, query_width + kv_width :] + value_shift)
            .reshape(block_rows, kv_heads, HD)
            .astype(jnp.bfloat16)
        )
        fresh_keys.append(new_key)
        fresh_vals.append(new_value)
        attended = attend(
            query,
            cache_keys,
            cache_vals,
            jnp.concatenate(fresh_keys, axis=0),
            jnp.concatenate(fresh_vals, axis=0),
            length,
            step,
        )
        return jnp.dot(
            lax.all_gather(attended, "rollout", axis=0, tiled=True),
            out_block,
            preferred_element_type=jnp.float32,
        )

    results = []
    whole_entering, whole_arriving = (
        lax.all_gather(entering[0], "tensor", axis=0, tiled=True),
        lax.all_gather(arriving, "tensor", axis=1, tiled=True),
    )
    current = whole_entering
    for step in range(BLOCKS):
        if step > 0:
            current = jnp.where(section == 0, whole_arriving[step - 1], handed)
        xf = current.astype(jnp.float32)
        squares = lax.psum(jnp.sum(xf * xf, axis=1), "rollout")
        normed_all = (xf * lax.rsqrt(squares / D + 1e-06)[:, None] * gain_block).astype(
            jnp.bfloat16
        )
        partial_sums = layer_core(normed_all, step)
        summed = lax.psum(partial_sums.astype(jnp.bfloat16), "tensor").astype(jnp.float32)
        updated = (xf + active * summed).astype(jnp.bfloat16)
        results.append(lax.dynamic_slice_in_dim(updated, tensor * token_rows, token_rows, 0))
        if step + 1 < BLOCKS:
            handed = from_behind(updated, "section", 1)
    section_out = jnp.stack(results)[None]
    new_rows = jnp.stack(
        [
            jnp.concatenate(fresh_keys, axis=0).reshape(-1, kv_width),
            jnp.concatenate(fresh_vals, axis=0).reshape(-1, kv_width),
        ],
        axis=1,
    )
    anchor = jnp.zeros((), jnp.int32)
    padded = jnp.concatenate([resident, jnp.zeros_like(new_rows)], axis=0)
    padded = lax.dynamic_update_slice(padded, new_rows, (length, anchor, anchor))
    kept_rows = jnp.arange(padded.shape[0], dtype=jnp.int32) < length + new_rows.shape[0]
    padded = jnp.where(kept_rows[:, None, None], padded, jnp.zeros_like(padded))
    page_count = padded.shape[0] // PAGE
    page_width = PAGE * 2 * kv_width
    pages = padded.reshape(page_count, page_width)
    dest_count = roll_count * section_count
    capacity = (page_count + dest_count - 1) // dest_count
    routing = block_table.reshape(dest_count, page_count, 2)
    targets = routing[:, :, 0]
    slot_ids = routing[:, :, 1]
    page_ids = jnp.arange(page_count, dtype=jnp.int32)
    before = page_ids[None, :] < page_ids[:, None]
    ranks = jnp.sum(
        ((targets[:, :, None] == targets[:, None, :]) & before[None]).astype(jnp.int32), axis=2
    )
    sources = jnp.arange(dest_count, dtype=jnp.int32)
    source_section = sources % section_count
    source_length = (
        resumed_pages[sources // section_count] * PAGE
        + (section_count - 1 - source_section) * BLOCK
        + BLOCKS * BLOCK
    )
    is_live = (page_ids[None, :] < (source_length // PAGE)[:, None]) & (
        section_active[source_section] > 0
    )[:, None]
    own_index = rollout * section_count + section
    columns = targets[own_index] * capacity + ranks[own_index]
    buffer_ids = jnp.arange(dest_count * capacity, dtype=jnp.int32)
    selector = ((buffer_ids[:, None] == columns[None, :]) & is_live[own_index][None, :]).astype(
        jnp.bfloat16
    )
    outgoing = jnp.dot(selector, pages, preferred_element_type=jnp.float32).astype(jnp.bfloat16)
    arrived = lax.all_to_all(
        outgoing.reshape(dest_count, capacity, page_width),
        ("rollout", "section"),
        split_axis=0,
        concat_axis=0,
        tiled=True,
    )
    arrived = arrived.reshape(dest_count * capacity, page_width)
    mine = (targets == own_index) & is_live
    slot_hit = ((slot_ids[:, :, None] == page_ids[None, None, :]) & mine[:, :, None]).astype(
        jnp.float32
    )
    column_of = sources[:, None] * capacity + ranks
    column_hit = (column_of[:, :, None] == buffer_ids[None, None, :]).astype(jnp.float32)
    placing = jnp.einsum("ips,ipc->sc", slot_hit, column_hit)
    pool = jnp.dot(
        placing.astype(jnp.bfloat16), arrived, preferred_element_type=jnp.float32
    ).astype(jnp.bfloat16)
    page_pool = pool.reshape(1, 1, page_count, PAGE, 2, kv_width)
    return (section_out, page_pool)


def solution(mesh):
    in_specs = (
        P("section", "tensor", "rollout"),
        P(None, "tensor", "rollout"),
        P("section", "rollout", "tensor"),
        P("section", "rollout", None, "tensor"),
        P("section", "tensor", "rollout"),
        P("section", "tensor"),
        P("section", None, "tensor"),
        P("section", "rollout"),
        P("rollout", "section", None, None, "tensor"),
        P(),
        P(),
        P(),
    )
    out_specs = (
        P("section", None, "tensor", "rollout"),
        P("rollout", "section", None, None, None, "tensor"),
    )
    return jax.shard_map(local, mesh=mesh, in_specs=in_specs, out_specs=out_specs, check_vma=False)
```

profile of v0, /device:TPU:13, one launch (start us, length us, event | category | flops | bytes accessed | tf_op | source)
XLA Modules:
  0.0 718.5 jit_solution(5743466451505818761)
XLA Ops:
  10.9 23.3 %psum.42 = f32[512]{0:T(512)S(1)} all-reduce(f32[512]{0:T(512)S(1)} %fusion.72), channel_id=1, replica_groups=mesh['rollout'=16,'section'=4,'tensor'=2] {'rollout'}, use_global_device_ids=true, to_apply=%region_1.0 | all-reduce | flops 512 | bytes 4096 | tf_op jit(solution)/shard_map/psum | solution.py:156
  36.7 5.1 convolution_convert_fusion.4
  43.7 7.4 %fusion.143 = (bf16[1120,1,512]{2,1,0:T(2,128)(2,1)}, bf16[1120,1,512]{2,1,0:T(2,128)(2,1)}) fusion(bf16[1120,2,512]{2,1,0:T(2,128)(2,1)} %bitcast.205), kind=kLoop, calls=%fused_computation.244 | loop fusion | bytes 4587520 | tf_op jit(solution)/shard_map/slice | solution.py:100
  51.1 5.0 copy.225
  57.5 5.0 copy.230
  64.0 64.6 %reduce-scatter.4.cloned.1.call-done = bf16[32,3072]{1,0:T(8,128)(2,1)} async-done(((bf16[512,3072]{1,0:T(8,128)(2,1)}), bf16[32,3072]{1,0:T(8,128)(2,1)}) %reduce-scatter.4.cloned.1.call-update) | async-done | bytes 196624 | tf_op jit(solution)/shard_map/reduce_scatter | solution.py:105
  137.5 44.9 %all-gather.6.cloned.1.call-done = bf16[512,2048]{1,0:T(8,128)(2,1)} async-done(((bf16[32,2048]{1,0:T(8,128)(2,1)}), bf16[512,2048]{1,0:T(8,128)(2,1)}) %all-gather.6.cloned.1.call-update) | async-done | bytes 2097168 | tf_op jit(solution)/shard_map/all_gather | solution.py:141
  188.0 25.1 %all-reduce.5.cloned.1.call-done = bf16[512,512]{1,0:T(8,128)(2,1)} async-done(((bf16[512,512]{1,0:T(8,128)(2,1)}), bf16[512,512]{1,0:T(8,128)(2,1)}) %all-reduce.5.cloned.1.call-update) | async-done | bytes 524304 | tf_op jit(solution)/shard_map/psum | solution.py:161
  215.2 4.0 collective-permute-start
  219.2 8.6 %all-gather.8.cloned.1.call-done = bf16[2,512,512]{2,1,0:T(8,128)(2,1)} async-done(((bf16[2,256,512]{2,1,0:T(8,128)(2,1)}), bf16[2,512,512]{2,1,0:T(8,128)(2,1)}) %all-gather.8.cloned.1.call-update) | async-done | bytes 1048592 | tf_op jit(solution)/shard_map/all_gather | solution.py:149
  231.8 23.6 %psum.44 = f32[512]{0:T(512)S(1)} all-reduce(f32[512]{0:T(512)S(1)} %get-tuple-element.4), channel_id=1, replica_groups=mesh['rollout'=16,'section'=4,'tensor'=2] {'rollout'}, use_global_device_ids=true, to_apply=%region_8.9 | all-reduce | flops 512 | bytes 4096 | tf_op jit(solution)/shard_map/psum | solution.py:156
  255.4 5.6 convolution_convert_fusion.3
  262.0 86.1 %reduce-scatter.6.cloned.1.call-done = bf16[32,3072]{1,0:T(8,128)(2,1)} async-done(((bf16[512,3072]{1,0:T(8,128)(2,1)}), bf16[32,3072]{1,0:T(8,128)(2,1)}) %reduce-scatter.6.cloned.1.call-update) | async-done | bytes 196624 | tf_op jit(solution)/shard_map/reduce_scatter | solution.py:105
  357.2 44.9 %all-gather.10.cloned.1.call-done = bf16[512,2048]{1,0:T(8,128)(2,1)} async-done(((bf16[32,2048]{1,0:T(8,128)(2,1)}), bf16[512,2048]{1,0:T(8,128)(2,1)}) %all-gather.10.cloned.1.call-update) | async-done | bytes 2097168 | tf_op jit(solution)/shard_map/all_gather | solution.py:141
  402.1 3.6 fusion.29
  405.9 27.0 %all-reduce.7.cloned.1.call-done = bf16[512,512]{1,0:T(8,128)(2,1)} async-done(((bf16[512,512]{1,0:T(8,128)(2,1)}), bf16[512,512]{1,0:T(8,128)(2,1)}) %all-reduce.7.cloned.1.call-update) | async-done | bytes 524304 | tf_op jit(solution)/shard_map/psum | solution.py:161
  438.2 11.1 %collective-permute-done.1 = bf16[512,512]{1,0:T(8,128)(2,1)S(1)} collective-permute-done((bf16[512,512]{1,0:T(8,128)(2,1)S(1)}, bf16[512,512]{1,0:T(8,128)(2,1)S(1)}, u32[]{:S(2)}, u32[]{:S(2)}) %collective-permute-start.1) | collective-permute-done | bytes 524320 | tf_op jit(solution)/shard_map/ppermute | solution.py:18
  451.5 23.6 %psum.46 = f32[512]{0:T(512)S(1)} all-reduce(f32[512]{0:T(512)S(1)} %get-tuple-element.2), channel_id=1, replica_groups=mesh['rollout'=16,'section'=4,'tensor'=2] {'rollout'}, use_global_device_ids=true, to_apply=%region_15.16 | all-reduce | flops 512 | bytes 4096 | tf_op jit(solution)/shard_map/psum | solution.py:156
  475.1 5.7 convolution_convert_fusion.2
  487.1 5.9 concatenate.95
  499.0 68.6 %reduce-scatter.8.cloned.1.call-done = bf16[32,3072]{1,0:T(8,128)(2,1)} async-done(((bf16[512,3072]{1,0:T(8,128)(2,1)}), bf16[32,3072]{1,0:T(8,128)(2,1)}) %reduce-scatter.8.cloned.1.call-update) | async-done | bytes 196624 | tf_op jit(solution)/shard_map/reduce_scatter | solution.py:105
  579.9 6.9 broadcast_select_fusion
  586.8 7.1 reshape.501
  593.8 5.0 fusion
  599.3 6.8 reduce.8
  606.1 7.9 %reshape.558 = bf16[64,2,16384]{2,1,0:T(2,128)(2,1)} reshape(bf16[64,32768]{1,0:T(8,128)(2,1)} %reduce.8) | data formatting | bytes 8388608
  614.1 9.8 %all-to-all-start = ((bf16[64,2,16384]{2,1,0:T(2,128)(2,1)}), bf16[64,2,16384]{2,1,0:T(2,128)(2,1)}, u32[]{:S(2)}, u32[]{:S(2)}) async-start(bf16[64,2,16384]{2,1,0:T(2,128)(2,1)} %reshape.558), calls=%async_computation.3 | async-start | bytes 8388608 | tf_op jit(solution)/shard_map/all_to_all | solution.py:209
  624.4 3.7 fusion.32
  629.8 41.6 %all-to-all-done = bf16[64,2,16384]{2,1,0:T(2,128)(2,1)} async-done(((bf16[64,2,16384]{2,1,0:T(2,128)(2,1)}), bf16[64,2,16384]{2,1,0:T(2,128)(2,1)}, u32[]{:S(2)}, u32[]{:S(2)}) %all-to-all-start) | async-done | bytes 4194336 | tf_op jit(solution)/shard_map/all_to_all | solution.py:209
  671.4 19.7 %reshape.559 = bf16[64,1,32768]{2,1,0:T(2,128)(2,1)} reshape(bf16[64,2,16384]{2,1,0:T(2,128)(2,1)} %all-to-all-done) | data formatting | bytes 8388608
  691.2 10.4 %convolution_convert_fusion.1 = bf16[38,32768]{1,0:T(8,128)(2,1)} fusion(bf16[64,1,32768]{2,1,0:T(2,128)(2,1)} %reshape.559, s32[64,38]{1,0:T(8,128)S(1)} %copy.259, s32[64,38]{1,0:T(8,128)S(1)} %copy-done.20, pred[64,38]{1,0:T(8,128)(4,1)S(1)} %fusion.111), kind=kOutput, calls=%fused_computation.3 | convolution fusion | flops 172800896 | bytes 6706560 | tf_op jit(solution)/shard_map/dot_general | solution.py:224
  701.6 7.1 reshape.504
  (249 shorter events, 77.6 us)
Async XLA Ops:
  7.2 175.2 %copy-start = (bf16[1,2048,512]{2,1,0:T(8,128)(2,1)S(1)}, bf16[1,2048,512]{2,1,0:T(8,128)(2,1)}, u32[]{:S(2)}) copy-start(bf16[1,2048,512]{2,1,0:T(8,128)(2,1)} %param.16) | copy-start | bytes 6291460
  7.2 121.4 %reduce-scatter.4.cloned.1.call-start = ((), (), s32[]{:S(2)}) async-start(), calls=%async_computation.4 | async-start | bytes 3342336 | tf_op jit(solution)/shard_map/reduce_scatter | solution.py:105
  8.1 33.7 %copy-start.48 = (f32[1,512]{1,0:T(1,128)}, f32[1,512]{1,0:T(1,128)S(1)}, u32[]{:S(2)}) copy-start(f32[1,512]{1,0:T(1,128)S(1)} %mul.471) | copy-start | bytes 6148
  10.7 31.1 %copy-start.2 = (bf16[1,512,512]{2,1,0:T(8,128)(2,1)}, bf16[1,512,512]{2,1,0:T(8,128)(2,1)S(1)}, u32[]{:S(2)}) copy-start(bf16[1,512,512]{2,1,0:T(8,128)(2,1)S(1)} %all-gather) | copy-start | bytes 1572868
  41.8 140.5 %all-gather.6.cloned.1.call-start = ((), (), s32[]{:S(2)}) async-start(), calls=%async_computation.5 | async-start | bytes 2228224 | tf_op jit(solution)/shard_map/all_gather | solution.py:141
  63.1 68.6 %copy-start.27 = (f32[1,1,512]{2,1,0:T(1,128)}, f32[1,1,512]{2,1,0:T(1,128)S(1)}, u32[]{:S(2)}) copy-start(f32[1,1,512]{2,1,0:T(1,128)S(1)} %get-tuple-element.38) | copy-start | bytes 6148
  63.1 68.6 %copy-start.30 = (f32[1,1,512]{2,1,0:T(1,128)}, f32[1,1,512]{2,1,0:T(1,128)S(1)}, u32[]{:S(2)}) copy-start(f32[1,1,512]{2,1,0:T(1,128)S(1)} %get-tuple-element.39) | copy-start | bytes 6148
  64.0 66.4 %copy-start.18 = (f32[32,64]{1,0:T(8,128)}, f32[32,64]{1,0:T(8,128)S(1)}, u32[]{:S(2)}) copy-start(f32[32,64]{1,0:T(8,128)S(1)} %get-tuple-element.53) | copy-start | bytes 24580
  64.0 66.4 %copy-start.19 = (f32[32,64]{1,0:T(8,128)}, f32[32,64]{1,0:T(8,128)S(1)}, u32[]{:S(2)}) copy-start(f32[32,64]{1,0:T(8,128)S(1)} %get-tuple-element.54) | copy-start | bytes 24580
  137.5 49.2 %copy-start.40 = (s32[4]{0:T(128)S(1)}, s32[4]{0:T(128)}, u32[]{:S(2)}) copy-start(s32[4]{0:T(128)} %param.22) | copy-start | bytes 52
  137.5 75.6 %all-reduce.5.cloned.1.call-start = ((), (), s32[]{:S(2)}) async-start(), calls=%async_computation.6 | async-start | bytes 1048576 | tf_op jit(solution)/shard_map/psum | solution.py:161
  186.0 69.4 %copy-start.49 = (f32[1,512]{1,0:T(1,128)S(1)}, f32[1,512]{1,0:T(1,128)}, u32[]{:S(2)}) copy-start(f32[1,512]{1,0:T(1,128)} %copy-done.48) | copy-start | bytes 6148
  186.0 41.8 %all-gather.8.cloned.1.call-start = ((), (), s32[]{:S(2)}) async-start(), calls=%async_computation.7 | async-start | bytes 1572864 | tf_op jit(solution)/shard_map/all_gather | solution.py:149
  186.6 161.5 %reduce-scatter.6.cloned.1.call-start = ((), (), s32[]{:S(2)}) async-start(), calls=%async_computation.8 | async-start | bytes 3342336 | tf_op jit(solution)/shard_map/reduce_scatter | solution.py:105
  215.2 14.6 %collective-permute-start = (bf16[512,512]{1,0:T(8,128)(2,1)}, bf16[512,512]{1,0:T(8,128)(2,1)}, u32[]{:S(2)}, u32[]{:S(2)}) collective-permute-start(bf16[512,512]{1,0:T(8,128)(2,1)} %fusion.75), channel_id=1, source_target_pairs={{0,2},{2,4},{4,6},{1,3},{3,5},{5,7},{8,10},{10,12},{12,14},{9,11},... | collective-permute-start | bytes 1572872 | tf_op jit(solution)/shard_map/ppermute | solution.py:18
  261.0 88.0 %copy-start.28 = (f32[1,1,512]{2,1,0:T(1,128)S(1)}, f32[1,1,512]{2,1,0:T(1,128)}, u32[]{:S(2)}) copy-start(f32[1,1,512]{2,1,0:T(1,128)} %copy-done.27) | copy-start | bytes 6148
  261.0 88.0 %copy-start.31 = (f32[1,1,512]{2,1,0:T(1,128)S(1)}, f32[1,1,512]{2,1,0:T(1,128)}, u32[]{:S(2)}) copy-start(f32[1,1,512]{2,1,0:T(1,128)} %copy-done.30) | copy-start | bytes 6148
  261.0 88.8 %copy-start.16 = (f32[32,64]{1,0:T(8,128)S(1)}, f32[32,64]{1,0:T(8,128)}, u32[]{:S(2)}) copy-start(f32[32,64]{1,0:T(8,128)} %get-tuple-element.51) | copy-start | bytes 24580
  261.0 88.8 %copy-start.17 = (f32[32,64]{1,0:T(8,128)S(1)}, f32[32,64]{1,0:T(8,128)}, u32[]{:S(2)}) copy-start(f32[32,64]{1,0:T(8,128)} %get-tuple-element.52) | copy-start | bytes 24580
  261.1 141.1 %all-gather.10.cloned.1.call-start = ((), (), s32[]{:S(2)}) async-start(), calls=%async_computation.9 | async-start | bytes 2228224 | tf_op jit(solution)/shard_map/all_gather | solution.py:141
  357.2 75.7 %all-reduce.7.cloned.1.call-start = ((), (), s32[]{:S(2)}) async-start(), calls=%async_computation.10 | async-start | bytes 1048576 | tf_op jit(solution)/shard_map/psum | solution.py:161
  405.8 69.3 %copy-start.50 = (f32[1,512]{1,0:T(1,128)S(1)}, f32[1,512]{1,0:T(1,128)}, u32[]{:S(2)}) copy-start(f32[1,512]{1,0:T(1,128)} %copy-done.48) | copy-start | bytes 6148
  405.8 161.8 %reduce-scatter.8.cloned.1.call-start = ((), (), s32[]{:S(2)}) async-start(), calls=%async_computation.11 | async-start | bytes 3342336 | tf_op jit(solution)/shard_map/reduce_scatter | solution.py:105
  435.0 14.3 %collective-permute-start.1 = (bf16[512,512]{1,0:T(8,128)(2,1)S(1)}, bf16[512,512]{1,0:T(8,128)(2,1)S(1)}, u32[]{:S(2)}, u32[]{:S(2)}) collective-permute-start(bf16[512,512]{1,0:T(8,128)(2,1)S(1)} %fusion.71), channel_id=1, source_target_pairs={{0,2},{2,4},{4,6},{1,3},{3,5},{5,7},{8,10},{10,12},{12,14},{9,11},... | collective-permute-start | bytes 1572872 | tf_op jit(solution)/shard_map/ppermute | solution.py:18
  480.9 143.5 %all-gather.12.cloned.1.call-start = ((), (), s32[]{:S(2)}) async-start(), calls=%async_computation.12 | async-start | bytes 2228224 | tf_op jit(solution)/shard_map/all_gather | solution.py:141
  487.0 81.5 %copy-start.29 = (f32[1,1,512]{2,1,0:T(1,128)S(1)}, f32[1,1,512]{2,1,0:T(1,128)}, u32[]{:S(2)}) copy-start(f32[1,1,512]{2,1,0:T(1,128)} %copy-done.27) | copy-start | bytes 6148
  487.0 81.6 %copy-start.32 = (f32[1,1,512]{2,1,0:T(1,128)S(1)}, f32[1,1,512]{2,1,0:T(1,128)}, u32[]{:S(2)}) copy-start(f32[1,1,512]{2,1,0:T(1,128)} %copy-done.30) | copy-start | bytes 6148
  487.0 82.3 %copy-start.14 = (f32[32,64]{1,0:T(8,128)S(1)}, f32[32,64]{1,0:T(8,128)}, u32[]{:S(2)}) copy-start(f32[32,64]{1,0:T(8,128)} %get-tuple-element.40) | copy-start | bytes 24580
  487.1 82.3 %copy-start.15 = (f32[32,64]{1,0:T(8,128)S(1)}, f32[32,64]{1,0:T(8,128)}, u32[]{:S(2)}) copy-start(f32[32,64]{1,0:T(8,128)} %get-tuple-element.41) | copy-start | bytes 24580
  614.1 57.3 %all-to-all-start = ((bf16[64,2,16384]{2,1,0:T(2,128)(2,1)}), bf16[64,2,16384]{2,1,0:T(2,128)(2,1)}, u32[]{:S(2)}, u32[]{:S(2)}) async-start(bf16[64,2,16384]{2,1,0:T(2,128)(2,1)} %reshape.558), calls=%async_computation.3 | async-start | bytes 8388608 | tf_op jit(solution)/shard_map/all_to_all | solution.py:209
  623.9 84.8 %all-reduce.9.cloned.1.call-start = ((), (), s32[]{:S(2)}) async-start(), calls=%async_computation.13 | async-start | bytes 1048576 | tf_op jit(solution)/shard_map/psum | solution.py:161
  629.8 61.3 %copy-start.20 = (s32[64,38]{1,0:T(8,128)S(1)}, s32[64,38]{1,0:T(8,128)}, u32[]{:S(2)}) copy-start(s32[64,38]{1,0:T(8,128)} %get-tuple-element.29) | copy-start | bytes 29188
  (35 other events, 117.4 us)
Sparse Core Ops, SparseCore 0:
  41.9 86.5 reduce-scatter.3
  137.6 44.7 all-gather.5
  186.1 26.8 all-reduce.4
  214.7 13.0 all-gather.7
  261.2 86.8 reduce-scatter.5
  357.3 44.7 all-gather.9
  405.9 26.8 all-reduce.6
  481.0 86.5 reduce-scatter.7
  579.1 44.8 all-gather.11
  628.2 28.4 all-reduce.8
where the time goes:
time: 730 us; the launch traced here: 718 us
  waiting for transfers between devices  425 us (58%)
  local copies, waits for them, and re-layouts  91.5 us (13%)
  blocking collectives  73.2 us (10%)
  matrix products  49.4 us (7%)
  other arithmetic  45.2 us (6%)
  starting transfers between devices  17.7 us (2%)
  between operations  16.4 us (2%)
    reduce_scatter x3, waiting for transfers between devices, layer_core(): lax.psum_scatter(jnp.dot(normed_all, weight_cat, preferred_element_type=j...  219 us
    all_gather x3, waiting for transfers between devices, layer_core(): lax.all_gather(attended, 'rollout', axis=0, tiled=True)  89.8 us
    psum x3, blocking collectives, local(): squares = lax.psum(jnp.sum(xf * xf, axis=1), 'rollout')  70.5 us
    psum x3, waiting for transfers between devices, local(): lax.psum(partial_sums.astype(jnp.bfloat16), 'tensor').astype(jnp.float32)  52.1 us
    all_to_all x1, waiting for transfers between devices, local(): lax.all_to_all(outgoing.reshape(dest_count, capacity, page_width), ('roll...  41.6 us
    unnamed x115, local copies, waits for them, and re-layouts  33.5 us
    dot_general x3, matrix products, layer_core(): jnp.dot(normed_all, weight_cat, preferred_element_type=jnp.float32)  16.5 us
  transfers between devices with their start and end apart: 13, of which 11 were waited for; matrix products, arithmetic and copies ran while one was open for 17% of the time, Pallas kernels for 0%

commit v1 on v0

v1 whole, which is shorter than its diff:
```python
import math

import jax
import jax.numpy as jnp
from jax import lax
from jax.experimental import pallas as pl
from jax.experimental.pallas import tpu as pltpu
from jax.sharding import Mesh, PartitionSpec as P

D = 8192
HD = 128
BLOCK = 32
BLOCKS = 3
PAGE = 32
SIDE = 4
SUMS = 128
ROLL = ("y", "x")
ALL = ("y", "x", "section", "tensor")
F32 = jnp.float32
BF16 = jnp.bfloat16


def dot(a, b):
    return jnp.dot(a, b, preferred_element_type=F32)


def params(*semantics):
    return pltpu.CompilerParams(
        vmem_limit_bytes=56 * 1024 * 1024, dimension_semantics=semantics or None
    )


def ring_routes(phase):
    routes = {}
    for shift in range(1, SIDE):
        route = []
        for y in range(SIDE):
            for x in range(SIDE):
                for s in range(SIDE):
                    for t in range(2):
                        along_x = t == phase
                        ty, tx = (y, (x + shift) % SIDE) if along_x else ((y + shift) % SIDE, x)
                        route.append(
                            (
                                ((y * SIDE + x) * SIDE + s) * 2 + t,
                                ((ty * SIDE + tx) * SIDE + s) * 2 + t,
                            )
                        )
        routes[shift] = route
    return routes


FIRST = ring_routes(0)
SECOND = ring_routes(1)


def ring(block, routes, shift):
    return lax.ppermute(block, ALL, routes[shift])


def split_sum(total):
    high = total.astype(BF16).astype(F32)
    low = total - high
    column = lax.broadcasted_iota(jnp.int32, (total.shape[0], SUMS), 1)
    return jnp.where(column == 0, high, jnp.where(column == 1, low, 0.0)).astype(BF16)


def project_kernel(rows_ref, x_ref, gain_ref, wq_ref, wkv_ref, o0, o1, o2, o3, scaled):
    outs = (o0, o1, o2, o3)
    j = pl.program_id(0)
    query_width = 2048

    @pl.when(j == 0)
    def _():
        gain = gain_ref[...].astype(F32)
        for first in range(SIDE):
            for second in range(SIDE):
                at = pl.multiple_of(rows_ref[first * SIDE + second], BLOCK)
                x = x_ref[pl.ds(at, BLOCK), :].astype(F32)
                low = second * BLOCK
                scaled[first, low : low + BLOCK, :] = (x * gain).astype(BF16)
                squares = jnp.sum(x * x, axis=1, keepdims=True)
                outs[first][low : low + BLOCK, 3072:] = split_sum(squares)

    @pl.when(j < 4)
    def _():
        for first in range(SIDE):
            at = pl.multiple_of(j * 512, 512)
            outs[first][:, pl.ds(at, 512)] = dot(scaled[first], wq_ref[...]).astype(BF16)

    @pl.when(j >= 4)
    def _():
        for first in range(SIDE):
            at = pl.multiple_of(j * 512, 512)
            outs[first][:, pl.ds(at, 512)] = dot(scaled[first], wkv_ref[...]).astype(BF16)


def project(rows, x, gain, wq, wkv):
    depth = x.shape[1]
    tokens = x.shape[0] // SIDE
    width = wq.shape[1] + wkv.shape[1] + SUMS
    whole = pl.BlockSpec((tokens, width), lambda j: (0, 0))
    return pl.pallas_call(
        project_kernel,
        grid=(6,),
        in_specs=[
            pl.BlockSpec(memory_space=pltpu.SMEM),
            pl.BlockSpec(x.shape, lambda j: (0, 0)),
            pl.BlockSpec((1, depth), lambda j: (0, 0)),
            pl.BlockSpec((depth, 512), lambda j: (0, jnp.minimum(j, 3))),
            pl.BlockSpec((depth, 512), lambda j: (0, jnp.maximum(j - 4, 0))),
        ],
        out_specs=[whole] * SIDE,
        out_shape=[jax.ShapeDtypeStruct((tokens, width), BF16)] * SIDE,
        scratch_shapes=[pltpu.VMEM((SIDE, tokens, depth), BF16)],
        compiler_params=params("arbitrary"),
        cost_estimate=pl.CostEstimate(
            flops=2 * x.shape[0] * depth * width, bytes_accessed=7 * 2**20, transcendentals=0
        ),
        name="project",
    )(rows, x, gain, wq, wkv)


def combine_kernel(a_ref, b_ref, c_ref, d_ref, o0, o1, o2, o3):
    outs = (o0, o1, o2, o3)
    last = pl.program_id(0) == pl.num_programs(0) - 1
    for second in range(SIDE):
        at = slice(second * BLOCK, (second + 1) * BLOCK)
        total = (
            a_ref[at, :].astype(F32)
            + b_ref[at, :].astype(F32)
            + c_ref[at, :].astype(F32)
            + d_ref[at, :].astype(F32)
        )
        outs[second][...] = total.astype(BF16)

        @pl.when(last)
        def _():
            squares = jnp.sum(total[:, -SUMS:], axis=1, keepdims=True)
            outs[second][:, total.shape[1] - SUMS :] = split_sum(squares)


def combine(blocks):
    tokens, width = blocks[0].shape
    step = 640
    return pl.pallas_call(
        combine_kernel,
        grid=(width // step,),
        in_specs=[pl.BlockSpec((tokens, step), lambda j: (0, j))] * SIDE,
        out_specs=[pl.BlockSpec((BLOCK, step), lambda j: (0, j))] * SIDE,
        out_shape=[jax.ShapeDtypeStruct((BLOCK, width), BF16)] * SIDE,
        compiler_params=params("arbitrary"),
        cost_estimate=pl.CostEstimate(
            flops=4 * tokens * width, bytes_accessed=10 * tokens * width, transcendentals=0
        ),
        name="combine",
    )(*blocks)


def attend_kernel(step, count, *refs):
    (length_ref, p0, p1, p2, p3, cos_ref, sin_ref, qb_ref, kvb_ref, cache_ref) = refs[:10]
    olds = refs[10 : 10 + 2 * step]
    out_ref, key_ref, val_ref = refs[10 + 2 * step :]
    length = length_ref[0]
    heads = count
    kv_width = heads * HD
    query_width = 4 * kv_width
    parts = (p0, p1, p2, p3)

    def columns(low, high):
        total = parts[0][:, low:high].astype(F32)
        for part in parts[1:]:
            total = total + part[:, low:high].astype(F32)
        return total

    squares = jnp.sum(columns(query_width + 2 * kv_width, p0.shape[1]), axis=1, keepdims=True)
    scale = lax.rsqrt(squares / D + 1e-06)
    cosine = cos_ref[...]
    sine = sin_ref[...]

    def rotate(values):
        return (values * cosine + pltpu.roll(values, HD // 2, 1) * sine).astype(BF16)

    context = cache_ref.shape[0]
    seen = lax.broadcasted_iota(jnp.int32, (1, context), 1) < length
    rows = 4 * BLOCK
    token = lax.broadcasted_iota(jnp.int32, (rows, BLOCK), 0) % BLOCK
    causal = lax.broadcasted_iota(jnp.int32, (rows, BLOCK), 1) <= token
    factor = 1.0 / math.sqrt(HD)

    def scores(q, k):
        return (
            lax.dot_general(q, k, (((1,), (1,)), ((), ())), preferred_element_type=F32) * factor
        )

    for head in range(heads):
        low = head * HD
        key = columns(query_width + low, query_width + low + HD) * scale
        key = rotate(key + kvb_ref[0:1, low : low + HD])
        val = columns(query_width + kv_width + low, query_width + kv_width + low + HD) * scale
        val = (val + kvb_ref[1:2, low : low + HD]).astype(BF16)
        key_ref[:, low : low + HD] = key
        val_ref[:, low : low + HD] = val
        group = []
        for g in range(4):
            at = (head * 4 + g) * HD
            query = columns(at, at + HD) * scale + qb_ref[0:1, at : at + HD]
            group.append(rotate(query))
        query = jnp.concatenate(group, axis=0)
        cached = jnp.where(seen, scores(query, cache_ref[:, low : low + HD]), -1e30)
        recent = [scores(query, olds[2 * i][:, low : low + HD]) for i in range(step)]
        recent.append(jnp.where(causal, scores(query, key), -1e30))
        peak = jnp.max(cached, axis=1, keepdims=True)
        for part in recent:
            peak = jnp.maximum(peak, jnp.max(part, axis=1, keepdims=True))
        powers = jnp.exp(cached - peak)
        total = jnp.sum(powers, axis=1, keepdims=True)
        mixed = dot(powers.astype(BF16), cache_ref[:, kv_width + low : kv_width + low + HD])
        for i, part in enumerate(recent):
            powers = jnp.exp(part - peak)
            total = total + jnp.sum(powers, axis=1, keepdims=True)
            value = olds[2 * i + 1][:, low : low + HD] if i < step else val
            mixed = mixed + dot(powers.astype(BF16), value)
        mixed = (mixed / total).astype(BF16)
        for g in range(4):
            at = (head * 4 + g) * HD
            out_ref[:, at : at + HD] = mixed[g * BLOCK : (g + 1) * BLOCK]


def attend(step, length, parts, cosine, sine, query_bias, keyval_bias, cache, olds):
    kv_width = keyval_bias.shape[1]
    heads = kv_width // HD
    vmem = pl.BlockSpec(memory_space=pltpu.VMEM)
    smem = pl.BlockSpec(memory_space=pltpu.SMEM)
    operands = [*parts, cosine, sine, query_bias, keyval_bias, cache, *olds]
    return pl.pallas_call(
        lambda *refs: attend_kernel(step, heads, *refs),
        in_specs=[smem] + [vmem] * len(operands),
        out_specs=[vmem] * 3,
        out_shape=[
            jax.ShapeDtypeStruct((BLOCK, 4 * kv_width), BF16),
            jax.ShapeDtypeStruct((BLOCK, kv_width), BF16),
            jax.ShapeDtypeStruct((BLOCK, kv_width), BF16),
        ],
        compiler_params=params(),
        cost_estimate=pl.CostEstimate(
            flops=4 * 4 * BLOCK * 1216 * kv_width,
            bytes_accessed=4 * 2**20,
            transcendentals=4 * BLOCK * heads * 1216,
        ),
        name="attend",
    )(length, *operands)


def mix_kernel(rows_ref, a0, a1, a2, a3, w_ref, mine_ref, other_ref, total):
    blocks = (a0, a1, a2, a3)
    k = pl.program_id(0)
    last = k == pl.num_programs(0) - 1
    half = mine_ref.shape[0]
    own = rows_ref[SIDE * SIDE] * half
    for first in range(SIDE):
        product = dot(blocks[first][...], w_ref[...])

        @pl.when(k == 0)
        def _():
            total[first] = product

        @pl.when(k > 0)
        def _():
            total[first] = total[first] + product

        @pl.when(last)
        def _():
            for second in range(SIDE):
                at = rows_ref[first * SIDE + second] - own
                here = (at >= 0) & (at < half)
                value = total[first, second * BLOCK : (second + 1) * BLOCK, :].astype(BF16)

                @pl.when(here)
                def _():
                    mine_ref[pl.ds(pl.multiple_of(at, BLOCK), BLOCK), :] = value

                @pl.when(jnp.logical_not(here))
                def _():
                    there = jnp.where(at < 0, at + half, at - half)
                    other_ref[pl.ds(pl.multiple_of(there, BLOCK), BLOCK), :] = value


def mix(rows, blocks, w):
    tokens, depth = blocks[0].shape
    width = w.shape[1]
    step = 512
    half = pl.BlockSpec((2 * tokens, width), lambda k: (0, 0))
    return pl.pallas_call(
        mix_kernel,
        grid=(depth // step,),
        in_specs=[pl.BlockSpec(memory_space=pltpu.SMEM)]
        + [pl.BlockSpec((tokens, step), lambda k: (0, k))] * SIDE
        + [pl.BlockSpec((step, width), lambda k: (k, 0))],
        out_specs=[half] * 2,
        out_shape=[jax.ShapeDtypeStruct((2 * tokens, width), BF16)] * 2,
        scratch_shapes=[pltpu.VMEM((SIDE, tokens, width), F32)],
        compiler_params=params("arbitrary"),
        cost_estimate=pl.CostEstimate(
            flops=8 * tokens * depth * width, bytes_accessed=5 * 2**20, transcendentals=0
        ),
        name="mix",
    )(rows, *blocks, w)


def ship_kernel(table_ref, resident_ref, f0, f1, f2, out_ref, sems):
    fresh = (f0, f1, f2)
    start = table_ref[38]

    def each(act):
        def body(p, carry):
            @pl.when(p < start)
            def _():
                act(resident_ref.at[p], p)

            return carry

        lax.fori_loop(0, resident_ref.shape[0], body, 0)
        for i in range(BLOCKS):
            act(fresh[i], start + i)

    def begin(source, p):
        pltpu.make_async_copy(source, out_ref.at[table_ref[p]], sems.at[p]).start()

    def end(source, p):
        pltpu.make_async_copy(source, out_ref.at[table_ref[p]], sems.at[p]).wait()

    each(begin)
    each(end)


def ship(table, resident, fresh, count):
    anywhere = pl.BlockSpec(memory_space=pl.ANY)
    return pl.pallas_call(
        ship_kernel,
        in_specs=[pl.BlockSpec(memory_space=pltpu.SMEM)] + [anywhere] * (1 + len(fresh)),
        out_specs=anywhere,
        out_shape=jax.ShapeDtypeStruct((count,) + resident.shape[1:], BF16),
        scratch_shapes=[pltpu.SemaphoreType.DMA((38,))],
        compiler_params=params(),
        cost_estimate=pl.CostEstimate(flops=0, bytes_accessed=5 * 2**20, transcendentals=0),
        name="ship",
    )(table, resident, *fresh)


def store_kernel(table_ref, arrived_ref, pool_ref, blank, sems):
    blank[...] = jnp.zeros_like(blank)

    def each(act):
        def body(q, carry):
            source = table_ref[q]

            @pl.when(source >= 0)
            def _():
                act(arrived_ref.at[jnp.maximum(source, 0)], q)

            @pl.when(source < 0)
            def _():
                act(blank, q)

            return carry

        lax.fori_loop(0, pool_ref.shape[0], body, 0)

    each(lambda source, q: pltpu.make_async_copy(source, pool_ref.at[q], sems.at[q]).start())
    each(lambda source, q: pltpu.make_async_copy(source, pool_ref.at[q], sems.at[q]).wait())


def store(table, arrived, slots):
    anywhere = pl.BlockSpec(memory_space=pl.ANY)
    return pl.pallas_call(
        store_kernel,
        in_specs=[pl.BlockSpec(memory_space=pltpu.SMEM), anywhere],
        out_specs=anywhere,
        out_shape=jax.ShapeDtypeStruct((slots,) + arrived.shape[1:], BF16),
        scratch_shapes=[
            pltpu.VMEM(arrived.shape[1:], BF16),
            pltpu.SemaphoreType.DMA((slots,)),
        ],
        compiler_params=params(),
        cost_estimate=pl.CostEstimate(flops=0, bytes_accessed=5 * 2**20, transcendentals=0),
        name="store",
    )(table, arrived)


def local(
    entering,
    arriving,
    w_query,
    w_keyval,
    w_out,
    query_bias,
    keyval_bias,
    norm_gain,
    resident_kv,
    resumed_pages,
    section_active,
    block_table,
):
    section_count = lax.axis_size("section")
    y = lax.axis_index("y")
    x = lax.axis_index("x")
    section = lax.axis_index("section")
    tensor = lax.axis_index("tensor")
    rollout = y * SIDE + x
    roll_count = SIDE * SIDE
    kv_width = w_keyval.shape[3]
    wq = w_query[0]
    wkv = w_keyval[0].reshape(w_keyval.shape[1], 2 * kv_width)
    w_mix = w_out[0]
    length = resumed_pages[rollout] * PAGE + (section_count - 1 - section) * BLOCK
    active = section_active[section].astype(F32)

    first = jnp.arange(SIDE, dtype=jnp.int32)[:, None]
    second = jnp.arange(SIDE, dtype=jnp.int32)[None, :]
    by_x = ((second + y) % SIDE) * SIDE + (first + x) % SIDE
    by_y = ((first + y) % SIDE) * SIDE + (second + x) % SIDE
    rows = (jnp.where(tensor == 0, by_x, by_y) * BLOCK).reshape(-1)
    rows = jnp.concatenate([rows, tensor[None]]).astype(jnp.int32)

    half = HD // 2
    freq = jnp.power(F32(1000000.0), -(jnp.arange(half, dtype=F32) * (2.0 / HD)))
    positions = length + jnp.arange(BLOCKS * BLOCK, dtype=jnp.int32)
    angle = positions.astype(F32)[:, None] * freq[None, :]
    cosine = jnp.concatenate([jnp.cos(angle), jnp.cos(angle)], axis=1)
    sine = jnp.concatenate([-jnp.sin(angle), jnp.sin(angle)], axis=1)

    resident = resident_kv[0, 0]
    cache = resident.reshape(resident.shape[0], 2 * kv_width)
    query_shift = query_bias.astype(F32)
    keyval_shift = keyval_bias[0].astype(F32)
    swap = [(0, 1), (1, 0)]
    relay = [(i, i + 1) for i in range(section_count - 1)]

    results = []
    olds = []
    current = entering[0]
    for step in range(BLOCKS):
        if step > 0:
            handed = lax.ppermute(results[-1], "section", relay)
            current = jnp.where(section == 0, arriving[step - 1], handed)
        whole = lax.all_gather(current, "tensor", axis=0, tiled=True)
        outs = project(rows, whole, norm_gain, wq, wkv)
        parts = [outs[0]] + [ring(outs[d], FIRST, d) for d in (2, 1, 3)]
        outs = combine(parts)
        parts = [outs[0]] + [ring(outs[d], SECOND, d) for d in (2, 1, 3)]
        at = step * BLOCK
        attended, key, val = attend(
            step,
            length[None],
            parts,
            cosine[at : at + BLOCK],
            sine[at : at + BLOCK],
            query_shift,
            keyval_shift,
            cache,
            olds,
        )
        olds += [key, val]
        gathered = jnp.concatenate(
            [attended] + [ring(attended, SECOND, (SIDE - d) % SIDE) for d in range(1, SIDE)]
        )
        blocks = [gathered] + [ring(gathered, FIRST, (SIDE - d) % SIDE) for d in range(1, SIDE)]
        mine, other = mix(rows, blocks, w_mix)
        theirs = lax.ppermute(other, "tensor", swap)
        summed = mine.astype(F32) + theirs.astype(F32)
        results.append((current.astype(F32) + active * summed).astype(BF16))
    section_out = jnp.stack(results)[None]

    dest_count = roll_count * section_count
    slots = block_table.shape[2]
    routing = block_table.reshape(dest_count, slots, 2)
    targets = routing[:, :, 0]
    slot_ids = routing[:, :, 1]
    own = rollout * section_count + section
    sources = jnp.arange(dest_count, dtype=jnp.int32)
    source_pages = (
        resumed_pages[:, None]
        + (section_count - 1 - jnp.arange(section_count, dtype=jnp.int32))[None, :]
        + BLOCKS
    )
    live_pages = jnp.where(section_active[None, :] > 0, source_pages, 0).reshape(-1)
    page_ids = jnp.arange(slots, dtype=jnp.int32)
    mine = (targets == own) & (page_ids[None, :] < live_pages[:, None])
    hit = mine[:, :, None] & (slot_ids[:, :, None] == page_ids)
    origin = jnp.max(jnp.where(hit, sources[:, None, None], -1), axis=(0, 1))
    sending = jnp.concatenate([targets[own], (length // PAGE)[None]]).astype(jnp.int32)

    pages = resident.reshape(-1, PAGE, 2, kv_width)
    fresh = [jnp.stack([olds[2 * i], olds[2 * i + 1]], axis=1) for i in range(BLOCKS)]
    outgoing = ship(sending, pages, fresh, dest_count)
    arrived = lax.all_to_all(outgoing, ROLL + ("section",), 0, 0, tiled=True)
    pool = store(origin, arrived, slots)
    return section_out, pool[None, None]


def solution(mesh):
    split = Mesh(mesh.devices.reshape(SIDE, SIDE, mesh.shape["section"], 2), ALL)
    in_specs = (
        P("section", "tensor", ROLL),
        P(None, "tensor", ROLL),
        P("section", ROLL, "tensor"),
        P("section", ROLL, None, "tensor"),
        P("section", "tensor", ROLL),
        P("section", "tensor"),
        P("section", None, "tensor"),
        P("section", ROLL),
        P(ROLL, "section", None, None, "tensor"),
        P(),
        P(),
        P(),
    )
    out_specs = (
        P("section", None, "tensor", ROLL),
        P(ROLL, "section", None, None, None, "tensor"),
    )
    return jax.shard_map(
        local, mesh=split, in_specs=in_specs, out_specs=out_specs, check_vma=False
    )
```

time: 730 us -> 487 us (0.67); the launches traced: 718 us -> 483 us
  waiting for transfers between devices: 425 us -> 173 us
  Pallas kernels: 0 us -> 191 us
  local copies, waits for them, and re-layouts: 91.5 us -> 16.6 us
  blocking collectives: 73.2 us -> 10.6 us
  starting transfers between devices: 17.7 us -> 78.2 us
  matrix products: 49.4 us -> 0 us
  other arithmetic: 45.2 us -> 11.1 us
  between operations: 16.4 us -> 2.59 us
    reduce_scatter x3 -> x0, waiting for transfers between devices: 219 us -> none  [layer_core(): lax.psum_scatter(jnp.dot(normed_all, weight_cat, preferred_element_type=j...]
    pallas_call x0 -> x14, Pallas kernels: none -> 191 us  [the longest x1 63.7 us: ship(): pl.pallas_call(ship_kernel, in_specs=[pl.BlockSpec(memory_space=pltpu.SME...]
    ppermute x2 -> x41, waiting for transfers between devices: 13.1 us -> 173 us  [the longest x36 160 us: ring(): return lax.ppermute(block, ALL, routes[shift])]
    all_gather x4 -> x0, waiting for transfers between devices: 98.4 us -> none  [the longest x3 89.8 us: layer_core(): lax.all_gather(attended, 'rollout', axis=0, tiled=True)]
    psum x3 -> x0, blocking collectives: 70.5 us -> none  [local(): squares = lax.psum(jnp.sum(xf * xf, axis=1), 'rollout')]
    psum x3 -> x0, waiting for transfers between devices: 52.1 us -> none  [local(): lax.psum(partial_sums.astype(jnp.bfloat16), 'tensor').astype(jnp.float32)]
    ppermute x2 -> x41, starting transfers between devices: 7.17 us -> 56.7 us  [the longest x36 40 us: ring(): return lax.ppermute(block, ALL, routes[shift])]
    dot_general x17 -> x0, matrix products: 49.4 us -> none  [the longest x3 16.5 us: layer_core(): jnp.dot(normed_all, weight_cat, preferred_element_type=jnp.float32)]
  transfers between devices with their start and end apart: 13 -> 42, of which waited for: 11 -> 30; matrix products, arithmetic and copies ran while one was open for 17% -> 3% of each run, Pallas kernels for 0% -> 1%
where the time goes in v1:
time: 487 us; the launch traced here: 483 us
  Pallas kernels  191 us (39%)
  waiting for transfers between devices  173 us (36%)
  starting transfers between devices  78.2 us (16%)
  local copies, waits for them, and re-layouts  16.6 us (3%)
  other arithmetic  11.1 us (2%)
  blocking collectives  10.6 us (2%)
    ppermute x36, waiting for transfers between devices, ring(): return lax.ppermute(block, ALL, routes[shift])  160 us
    pallas_call x1, Pallas kernels, ship(): pl.pallas_call(ship_kernel, in_specs=[pl.BlockSpec(memory_space=pltpu.SME...  63.7 us
    pallas_call x1, Pallas kernels, store(): pl.pallas_call(store_kernel, in_specs=[pl.BlockSpec(memory_space=pltpu.SM...  55.7 us
    ppermute x36, starting transfers between devices, ring(): return lax.ppermute(block, ALL, routes[shift])  40 us
    pallas_call x3, Pallas kernels, project(): pl.pallas_call(project_kernel, grid=(6,), in_specs=[pl.BlockSpec(memory_s...  22.3 us
    all_to_all x1, starting transfers between devices, local(): arrived = lax.all_to_all(outgoing, ROLL + ('section',), 0, 0, tiled=True)  21.6 us
    pallas_call x3, Pallas kernels, mix(): pl.pallas_call(mix_kernel, grid=(depth // step,), in_specs=[pl.BlockSpec(...  20.1 us
    pallas_call x3, Pallas kernels, attend(): pl.pallas_call(lambda *refs: attend_kernel(step, heads, *refs), in_specs=...  14.9 us
  transfers between devices with their start and end apart: 42, of which 30 were waited for; matrix products, arithmetic and copies ran while one was open for 3% of the time, Pallas kernels for 1%

profile of v1, /device:TPU:13, one launch (start us, length us, event | category | flops | bytes accessed | tf_op | source)
XLA Modules:
  0.0 483.1 jit_solution(4994630417003813569)
XLA Ops:
  0.8 4.4 all-gather
  8.2 7.5 %project.3 = (bf16[128,3200]{1,0:T(8,128)(2,1)}, bf16[128,3200]{1,0:T(8,128)(2,1)}, bf16[128,3200]{1,0:T(8,128)(2,1)}, bf16[128,3200]{1,0:T(8,128)(2,1)}) custom-call(s32[17]{0:T(128)} %pad_add_fusion.rows_ref, bf16[512,512]{1,0:T(8,128)(2,1)} %bitcast.59, bf16[1,512]{1,0:T(2,128)(2,1)} %gain_ref.5, bf16[512,2048]{1,0:T(8,128)(2,1)} %bitcast.69, ...), custom_call_target="tpu_custom_call" | custom-call | flops 1677721600 | bytes 7340032 | tf_op jit(solution)/shard_map/project/pallas_call | solution.py:103
  24.1 4.9 %collective-permute-done.b_ref = bf16[128,3200]{1,0:T(8,128)(2,1)S(1)} collective-permute-done((bf16[128,3200]{1,0:T(8,128)(2,1)}, bf16[128,3200]{1,0:T(8,128)(2,1)S(1)}, u32[]{:S(2)}, u32[]{:S(2)}) %collective-permute-start) | collective-permute-done | bytes 819232 | tf_op jit(solution)/shard_map/ppermute | solution.py:58
  29.0 8.7 %collective-permute-done.1.c_ref = bf16[128,3200]{1,0:T(8,128)(2,1)} collective-permute-done((bf16[128,3200]{1,0:T(8,128)(2,1)}, bf16[128,3200]{1,0:T(8,128)(2,1)}, u32[]{:S(2)}, u32[]{:S(2)}) %collective-permute-start.1) | collective-permute-done | bytes 819232 | tf_op jit(solution)/shard_map/ppermute | solution.py:58
  37.7 4.9 %combine.3 = (bf16[32,3200]{1,0:T(8,128)(2,1)}, bf16[32,3200]{1,0:T(8,128)(2,1)}, bf16[32,3200]{1,0:T(8,128)(2,1)}, bf16[32,3200]{1,0:T(8,128)(2,1)}) custom-call(bf16[128,3200]{1,0:T(8,128)(2,1)} %get-tuple-element.41.a_ref, bf16[128,3200]{1,0:T(8,128)(2,1)} %copy-done.8, bf16[128,3200]{1,0:T(8,128)(2,1)} %collective-permute-done.1.c_ref, ...), custom_call_target="tpu_custom_call" | custom-call | flops 1638400 | bytes 4096000 | tf_op jit(solution)/shard_map/combine/pallas_call | solution.py:146
  51.7 4.8 attend.3
  67.8 4.7 collective-permute-done.11.a3
  74.0 5.8 %collective-permute-done.9.a1 = bf16[128,2048]{1,0:T(8,128)(2,1)S(1)} collective-permute-done((bf16[128,2048]{1,0:T(8,128)(2,1)S(1)}, bf16[128,2048]{1,0:T(8,128)(2,1)S(1)}, u32[]{:S(2)}, u32[]{:S(2)}) %collective-permute-start.9) | collective-permute-done | bytes 524320 | tf_op jit(solution)/shard_map/ppermute | solution.py:58
  80.6 6.7 %mix.3 = (bf16[256,512]{1,0:T(8,128)(2,1)}, bf16[256,512]{1,0:T(8,128)(2,1)}) custom-call(s32[17]{0:T(128)} %pad_add_fusion.rows_ref, bf16[128,2048]{1,0:T(8,128)(2,1)} %copy-done.2, bf16[128,2048]{1,0:T(8,128)(2,1)} %copy-done.19, bf16[128,2048]{1,0:T(8,128)(2,1)} %copy-done.17, bf16[128,2048]{1,0:T(8,128)(2,1)} %copy-done.15, bf16[2048,512]{1,0:T(8,128)(2,1)} %bitcast.47), custom_call_target="tpu_custom_call" | custom-call | flops 1073741824 | bytes 5242880 | tf_op jit(solution)/shard_map/mix/pallas_call | solution.py:294
  87.4 4.3 collective-permute-start.12
  97.7 5.3 %collective-permute-done.13 = bf16[256,512]{1,0:T(8,128)(2,1)S(1)} collective-permute-done((bf16[256,512]{1,0:T(8,128)(2,1)S(1)}, bf16[256,512]{1,0:T(8,128)(2,1)S(1)}, u32[]{:S(2)}, u32[]{:S(2)}) %collective-permute-start.13) | collective-permute-done | bytes 262176 | tf_op jit(solution)/shard_map/ppermute | solution.py:445
  106.2 7.4 %project.4 = (bf16[128,3200]{1,0:T(8,128)(2,1)}, bf16[128,3200]{1,0:T(8,128)(2,1)}, bf16[128,3200]{1,0:T(8,128)(2,1)}, bf16[128,3200]{1,0:T(8,128)(2,1)}) custom-call(s32[17]{0:T(128)} %pad_add_fusion.rows_ref, bf16[512,512]{1,0:T(8,128)(2,1)} %all_gather.10.x_ref, bf16[1,512]{1,0:T(2,128)(2,1)} %gain_ref.5, bf16[512,2048]{1,0:T(8,128)(2,1)} %bitcast.70, ...), custom_call_target="tpu_custom_call" | custom-call | flops 1677721600 | bytes 7340032 | tf_op jit(solution)/shard_map/project/pallas_call | solution.py:103
  117.1 9.6 %collective-permute-done.14.b_ref = bf16[128,3200]{1,0:T(8,128)(2,1)S(1)} collective-permute-done((bf16[128,3200]{1,0:T(8,128)(2,1)}, bf16[128,3200]{1,0:T(8,128)(2,1)S(1)}, u32[]{:S(2)}, u32[]{:S(2)}) %collective-permute-start.14) | collective-permute-done | bytes 819232 | tf_op jit(solution)/shard_map/ppermute | solution.py:58
  126.8 8.9 %collective-permute-done.15.c_ref = bf16[128,3200]{1,0:T(8,128)(2,1)S(1)} collective-permute-done((bf16[128,3200]{1,0:T(8,128)(2,1)}, bf16[128,3200]{1,0:T(8,128)(2,1)S(1)}, u32[]{:S(2)}, u32[]{:S(2)}) %collective-permute-start.15) | collective-permute-done | bytes 819232 | tf_op jit(solution)/shard_map/ppermute | solution.py:58
  136.8 4.9 %combine.4 = (bf16[32,3200]{1,0:T(8,128)(2,1)}, bf16[32,3200]{1,0:T(8,128)(2,1)}, bf16[32,3200]{1,0:T(8,128)(2,1)}, bf16[32,3200]{1,0:T(8,128)(2,1)}) custom-call(bf16[128,3200]{1,0:T(8,128)(2,1)} %get-tuple-element.52.a_ref, bf16[128,3200]{1,0:T(8,128)(2,1)} %copy-done.9, bf16[128,3200]{1,0:T(8,128)(2,1)} %copy-done.10, bf16[128,3200]{1,0:T(8,128)(2,1)} %copy-done.11), custom_call_target="tpu_custom_call" | custom-call | flops 1638400 | bytes 4096000 | tf_op jit(solution)/shard_map/combine/pallas_call | solution.py:146
  151.3 5.0 %attend.4 = (bf16[32,2048]{1,0:T(8,128)(2,1)}, bf16[32,512]{1,0:T(8,128)(2,1)}, bf16[32,512]{1,0:T(8,128)(2,1)}) custom-call(s32[1]{0:T(128)} %bitcast.4.refs_0_, bf16[32,3200]{1,0:T(8,128)(2,1)} %get-tuple-element.56.refs_1_, bf16[32,3200]{1,0:T(8,128)(2,1)} %copy-done.28, bf16[32,3200]{1,0:T(8,128)(2,1)} %copy-done.30, bf16[32,3200]{1,0:T(8,128)(2,1)} %copy-done.32, ...), custom_call_target="tpu_custom_call" | custom-call | flops 318767104 | bytes 4194304 | tf_op jit(solution)/shard_map/attend/pallas_call | solution.py:236
  167.5 5.0 %collective-permute-done.25.a3 = bf16[128,2048]{1,0:T(8,128)(2,1)S(1)} collective-permute-done((bf16[128,2048]{1,0:T(8,128)(2,1)S(1)}, bf16[128,2048]{1,0:T(8,128)(2,1)S(1)}, u32[]{:S(2)}, u32[]{:S(2)}) %collective-permute-start.25) | collective-permute-done | bytes 524320 | tf_op jit(solution)/shard_map/ppermute | solution.py:58
  174.5 5.8 %collective-permute-done.23.a1 = bf16[128,2048]{1,0:T(8,128)(2,1)S(1)} collective-permute-done((bf16[128,2048]{1,0:T(8,128)(2,1)S(1)}, bf16[128,2048]{1,0:T(8,128)(2,1)S(1)}, u32[]{:S(2)}, u32[]{:S(2)}) %collective-permute-start.23) | collective-permute-done | bytes 524320 | tf_op jit(solution)/shard_map/ppermute | solution.py:58
  181.1 6.7 %mix.4 = (bf16[256,512]{1,0:T(8,128)(2,1)}, bf16[256,512]{1,0:T(8,128)(2,1)}) custom-call(s32[17]{0:T(128)} %pad_add_fusion.rows_ref, bf16[128,2048]{1,0:T(8,128)(2,1)} %copy-done.3, bf16[128,2048]{1,0:T(8,128)(2,1)} %copy-done.20, bf16[128,2048]{1,0:T(8,128)(2,1)} %copy-done.18, bf16[128,2048]{1,0:T(8,128)(2,1)} %copy-done.16, bf16[2048,512]{1,0:T(8,128)(2,1)} %bitcast.48), custom_call_target="tpu_custom_call" | custom-call | flops 1073741824 | bytes 5242880 | tf_op jit(solution)/shard_map/mix/pallas_call | solution.py:294
  187.8 4.7 collective-permute-start.26
  199.1 5.3 %collective-permute-done.27 = bf16[256,512]{1,0:T(8,128)(2,1)S(1)} collective-permute-done((bf16[256,512]{1,0:T(8,128)(2,1)S(1)}, bf16[256,512]{1,0:T(8,128)(2,1)S(1)}, u32[]{:S(2)}, u32[]{:S(2)}) %collective-permute-start.27) | collective-permute-done | bytes 262176 | tf_op jit(solution)/shard_map/ppermute | solution.py:445
  207.5 7.4 %project.5 = (bf16[128,3200]{1,0:T(8,128)(2,1)}, bf16[128,3200]{1,0:T(8,128)(2,1)}, bf16[128,3200]{1,0:T(8,128)(2,1)}, bf16[128,3200]{1,0:T(8,128)(2,1)}) custom-call(s32[17]{0:T(128)} %pad_add_fusion.rows_ref, bf16[512,512]{1,0:T(8,128)(2,1)} %all_gather.11.x_ref, bf16[1,512]{1,0:T(2,128)(2,1)} %gain_ref.5, bf16[512,2048]{1,0:T(8,128)(2,1)} %bitcast.71, ...), custom_call_target="tpu_custom_call" | custom-call | flops 1677721600 | bytes 7340032 | tf_op jit(solution)/shard_map/project/pallas_call | solution.py:103
  219.6 8.7 %collective-permute-done.28.b_ref = bf16[128,3200]{1,0:T(8,128)(2,1)S(1)} collective-permute-done((bf16[128,3200]{1,0:T(8,128)(2,1)}, bf16[128,3200]{1,0:T(8,128)(2,1)S(1)}, u32[]{:S(2)}, u32[]{:S(2)}) %collective-permute-start.28) | collective-permute-done | bytes 819232 | tf_op jit(solution)/shard_map/ppermute | solution.py:58
  228.3 8.1 %collective-permute-done.29.c_ref = bf16[128,3200]{1,0:T(8,128)(2,1)S(1)} collective-permute-done((bf16[128,3200]{1,0:T(8,128)(2,1)}, bf16[128,3200]{1,0:T(8,128)(2,1)S(1)}, u32[]{:S(2)}, u32[]{:S(2)}) %collective-permute-start.29) | collective-permute-done | bytes 819232 | tf_op jit(solution)/shard_map/ppermute | solution.py:58
  237.9 4.9 %combine.5 = (bf16[32,3200]{1,0:T(8,128)(2,1)}, bf16[32,3200]{1,0:T(8,128)(2,1)}, bf16[32,3200]{1,0:T(8,128)(2,1)}, bf16[32,3200]{1,0:T(8,128)(2,1)}) custom-call(bf16[128,3200]{1,0:T(8,128)(2,1)} %get-tuple-element.65.a_ref, bf16[128,3200]{1,0:T(8,128)(2,1)} %copy-done.5, bf16[128,3200]{1,0:T(8,128)(2,1)} %copy-done.6, bf16[128,3200]{1,0:T(8,128)(2,1)} %copy-done.7), custom_call_target="tpu_custom_call" | custom-call | flops 1638400 | bytes 4096000 | tf_op jit(solution)/shard_map/combine/pallas_call | solution.py:146
  252.4 5.1 %attend.5 = (bf16[32,2048]{1,0:T(8,128)(2,1)}, bf16[32,512]{1,0:T(8,128)(2,1)}, bf16[32,512]{1,0:T(8,128)(2,1)}) custom-call(s32[1]{0:T(128)} %bitcast.4.refs_0_, bf16[32,3200]{1,0:T(8,128)(2,1)} %get-tuple-element.69.refs_1_, bf16[32,3200]{1,0:T(8,128)(2,1)} %copy-done.24, bf16[32,3200]{1,0:T(8,128)(2,1)} %copy-done.25, bf16[32,3200]{1,0:T(8,128)(2,1)} %copy-done.26, ...), custom_call_target="tpu_custom_call" | custom-call | flops 318767104 | bytes 4194304 | tf_op jit(solution)/shard_map/attend/pallas_call | solution.py:236
  259.9 63.7 %ship.1 = bf16[64,32,2,512]{3,2,1,0:T(2,128)(2,1)} custom-call(s32[39]{0:T(128)} %pad_add_fusion.1.table_ref, bf16[35,32,2,512]{3,2,1,0:T(2,128)(2,1)} %bitcast.50, bf16[32,2,512]{2,1,0:T(2,128)(2,1)} %pad_maximum_fusion.f0, bf16[32,2,512]{2,1,0:T(2,128)(2,1)} %pad_maximum_fusion.1.f1, bf16[32,2,512]{2,1,0:T(2,128)(2,1)} %pad_maximum_fusion.2.f2), custom_call_target="tpu_custom_call" | custom-call | bytes 5242880 | tf_op jit(solution)/shard_map/ship/pallas_call | solution.py:339
  323.6 21.6 %all-to-all-start = ((bf16[64,32,2,512]{3,2,1,0:T(2,128)(2,1)}), bf16[64,32,2,512]{3,2,1,0:T(2,128)(2,1)}, u32[]{:S(2)}, u32[]{:S(2)}) async-start(bf16[64,32,2,512]{3,2,1,0:T(2,128)(2,1)} %ship.1), calls=%async_computation | async-start | bytes 8388608 | tf_op jit(solution)/shard_map/all_to_all | solution.py:497
  347.6 52.2 %collective-permute-done.34 = bf16[32,2048]{1,0:T(8,128)(2,1)S(1)} collective-permute-done((bf16[32,2048]{1,0:T(8,128)(2,1)S(1)}, bf16[32,2048]{1,0:T(8,128)(2,1)S(1)}, u32[]{:S(2)}, u32[]{:S(2)}) %collective-permute-start.34) | collective-permute-done | bytes 131104 | tf_op jit(solution)/shard_map/ppermute | solution.py:58
  410.6 5.3 %collective-permute-done.37.a1 = bf16[128,2048]{1,0:T(8,128)(2,1)S(1)} collective-permute-done((bf16[128,2048]{1,0:T(8,128)(2,1)S(1)}, bf16[128,2048]{1,0:T(8,128)(2,1)S(1)}, u32[]{:S(2)}, u32[]{:S(2)}) %collective-permute-start.37) | collective-permute-done | bytes 524320 | tf_op jit(solution)/shard_map/ppermute | solution.py:58
  416.7 6.7 %mix.5 = (bf16[256,512]{1,0:T(8,128)(2,1)}, bf16[256,512]{1,0:T(8,128)(2,1)}) custom-call(s32[17]{0:T(128)} %pad_add_fusion.rows_ref, bf16[128,2048]{1,0:T(8,128)(2,1)} %copy-done.4, bf16[128,2048]{1,0:T(8,128)(2,1)} %copy-done.14, bf16[128,2048]{1,0:T(8,128)(2,1)} %copy-done.13, bf16[128,2048]{1,0:T(8,128)(2,1)} %copy-done.12, bf16[2048,512]{1,0:T(8,128)(2,1)} %bitcast.49), custom_call_target="tpu_custom_call" | custom-call | flops 1073741824 | bytes 5242880 | tf_op jit(solution)/shard_map/mix/pallas_call | solution.py:294
  427.2 55.7 %store.1 = bf16[38,32,2,512]{3,2,1,0:T(2,128)(2,1)} custom-call(s32[38]{0:T(128)} %select_reduce_fusion.table_ref, bf16[64,32,2,512]{3,2,1,0:T(2,128)(2,1)} %all-to-all-done.arrived_ref), custom_call_target="tpu_custom_call" | custom-call | bytes 5242880 | tf_op jit(solution)/shard_map/store/pallas_call | solution.py:376
  (204 shorter events, 116.0 us)
Async XLA Ops:
  15.7 13.2 %collective-permute-start = (bf16[128,3200]{1,0:T(8,128)(2,1)}, bf16[128,3200]{1,0:T(8,128)(2,1)S(1)}, u32[]{:S(2)}, u32[]{:S(2)}) collective-permute-start(bf16[128,3200]{1,0:T(8,128)(2,1)} %get-tuple-element.42), channel_id=1, source_target_pairs={{0,16},{1,65},{2,18},{3,67},{4,20},{5,69},{6,22},{7,71},{8,24},{9,... | collective-permute-start | bytes 2457608 | tf_op jit(solution)/shard_map/ppermute | solution.py:58
  17.8 19.9 %collective-permute-start.1 = (bf16[128,3200]{1,0:T(8,128)(2,1)}, bf16[128,3200]{1,0:T(8,128)(2,1)}, u32[]{:S(2)}, u32[]{:S(2)}) collective-permute-start(bf16[128,3200]{1,0:T(8,128)(2,1)} %get-tuple-element.43), channel_id=1, source_target_pairs={{0,8},{1,33},{2,10},{3,35},{4,12},{5,37},{6,14},{7,39},{8,16},{9,4... | collective-permute-start | bytes 2457608 | tf_op jit(solution)/shard_map/ppermute | solution.py:58
  17.8 19.9 %collective-permute-start.2 = (bf16[128,3200]{1,0:T(8,128)(2,1)}, bf16[128,3200]{1,0:T(8,128)(2,1)}, u32[]{:S(2)}, u32[]{:S(2)}) collective-permute-start(bf16[128,3200]{1,0:T(8,128)(2,1)} %get-tuple-element.44), channel_id=1, source_target_pairs={{0,24},{1,97},{2,26},{3,99},{4,28},{5,101},{6,30},{7,103},{8,0},{9... | collective-permute-start | bytes 2457608 | tf_op jit(solution)/shard_map/ppermute | solution.py:58
  42.6 6.7 %collective-permute-start.3 = (bf16[32,3200]{1,0:T(8,128)(2,1)}, bf16[32,3200]{1,0:T(8,128)(2,1)S(1)}, u32[]{:S(2)}, u32[]{:S(2)}) collective-permute-start(bf16[32,3200]{1,0:T(8,128)(2,1)} %get-tuple-element.46), channel_id=1, source_target_pairs={{0,64},{1,17},{2,66},{3,19},{4,68},{5,21},{6,70},{7,23},{8,72},{9,... | collective-permute-start | bytes 614408 | tf_op jit(solution)/shard_map/ppermute | solution.py:58
  43.2 7.7 %collective-permute-start.4 = (bf16[32,3200]{1,0:T(8,128)(2,1)}, bf16[32,3200]{1,0:T(8,128)(2,1)S(1)}, u32[]{:S(2)}, u32[]{:S(2)}) collective-permute-start(bf16[32,3200]{1,0:T(8,128)(2,1)} %get-tuple-element.47), channel_id=1, source_target_pairs={{0,32},{1,9},{2,34},{3,11},{4,36},{5,13},{6,38},{7,15},{8,40},{9,1... | collective-permute-start | bytes 614408 | tf_op jit(solution)/shard_map/ppermute | solution.py:58
  56.5 7.6 %collective-permute-start.8 = (bf16[32,2048]{1,0:T(8,128)(2,1)}, bf16[32,2048]{1,0:T(8,128)(2,1)S(1)}, u32[]{:S(2)}, u32[]{:S(2)}) collective-permute-start(bf16[32,2048]{1,0:T(8,128)(2,1)} %get-tuple-element.49), channel_id=1, source_target_pairs={{0,32},{1,9},{2,34},{3,11},{4,36},{5,13},{6,38},{7,15},{8,40},{9,1... | collective-permute-start | bytes 393224 | tf_op jit(solution)/shard_map/ppermute | solution.py:58
  64.1 8.4 %collective-permute-start.11 = (bf16[128,2048]{1,0:T(8,128)(2,1)S(1)}, bf16[128,2048]{1,0:T(8,128)(2,1)S(1)}, u32[]{:S(2)}, u32[]{:S(2)}) collective-permute-start(bf16[128,2048]{1,0:T(8,128)(2,1)S(1)} %constant_dynamic-update-slice_fusion.a0), channel_id=1, source_target_pairs={{0,8},{1,33},{2,10},{3,35},{4,12},{5,37},{6,14},{7,39},{8,16},{9,4... | collective-permute-start | bytes 1572872 | tf_op jit(solution)/shard_map/ppermute | solution.py:58
  64.4 9.6 %collective-permute-start.10 = (bf16[128,2048]{1,0:T(8,128)(2,1)S(1)}, bf16[128,2048]{1,0:T(8,128)(2,1)S(1)}, u32[]{:S(2)}, u32[]{:S(2)}) collective-permute-start(bf16[128,2048]{1,0:T(8,128)(2,1)S(1)} %constant_dynamic-update-slice_fusion.a0), channel_id=1, source_target_pairs={{0,16},{1,65},{2,18},{3,67},{4,20},{5,69},{6,22},{7,71},{8,24},{9,... | collective-permute-start | bytes 1572872 | tf_op jit(solution)/shard_map/ppermute | solution.py:58
  66.5 13.3 %collective-permute-start.9 = (bf16[128,2048]{1,0:T(8,128)(2,1)S(1)}, bf16[128,2048]{1,0:T(8,128)(2,1)S(1)}, u32[]{:S(2)}, u32[]{:S(2)}) collective-permute-start(bf16[128,2048]{1,0:T(8,128)(2,1)S(1)} %constant_dynamic-update-slice_fusion.a0), channel_id=1, source_target_pairs={{0,24},{1,97},{2,26},{3,99},{4,28},{5,101},{6,30},{7,103},{8,0},{9... | collective-permute-start | bytes 1572872 | tf_op jit(solution)/shard_map/ppermute | solution.py:58
  94.1 8.9 %collective-permute-start.13 = (bf16[256,512]{1,0:T(8,128)(2,1)S(1)}, bf16[256,512]{1,0:T(8,128)(2,1)S(1)}, u32[]{:S(2)}, u32[]{:S(2)}) collective-permute-start(bf16[256,512]{1,0:T(8,128)(2,1)S(1)} %fusion.1), channel_id=1, source_target_pairs={{0,2},{2,4},{4,6},{1,3},{3,5},{5,7},{8,10},{10,12},{12,14},{9,11},... | collective-permute-start | bytes 786440 | tf_op jit(solution)/shard_map/ppermute | solution.py:445
  113.5 13.2 %collective-permute-start.14 = (bf16[128,3200]{1,0:T(8,128)(2,1)}, bf16[128,3200]{1,0:T(8,128)(2,1)S(1)}, u32[]{:S(2)}, u32[]{:S(2)}) collective-permute-start(bf16[128,3200]{1,0:T(8,128)(2,1)} %get-tuple-element.53), channel_id=1, source_target_pairs={{0,16},{1,65},{2,18},{3,67},{4,20},{5,69},{6,22},{7,71},{8,24},{9,... | collective-permute-start | bytes 2457608 | tf_op jit(solution)/shard_map/ppermute | solution.py:58
  115.7 20.0 %collective-permute-start.15 = (bf16[128,3200]{1,0:T(8,128)(2,1)}, bf16[128,3200]{1,0:T(8,128)(2,1)S(1)}, u32[]{:S(2)}, u32[]{:S(2)}) collective-permute-start(bf16[128,3200]{1,0:T(8,128)(2,1)} %get-tuple-element.54), channel_id=1, source_target_pairs={{0,8},{1,33},{2,10},{3,35},{4,12},{5,37},{6,14},{7,39},{8,16},{9,4... | collective-permute-start | bytes 2457608 | tf_op jit(solution)/shard_map/ppermute | solution.py:58
  116.5 19.1 %collective-permute-start.16 = (bf16[128,3200]{1,0:T(8,128)(2,1)}, bf16[128,3200]{1,0:T(8,128)(2,1)S(1)}, u32[]{:S(2)}, u32[]{:S(2)}) collective-permute-start(bf16[128,3200]{1,0:T(8,128)(2,1)} %get-tuple-element.55), channel_id=1, source_target_pairs={{0,24},{1,97},{2,26},{3,99},{4,28},{5,101},{6,30},{7,103},{8,0},{9... | collective-permute-start | bytes 2457608 | tf_op jit(solution)/shard_map/ppermute | solution.py:58
  141.7 6.7 %collective-permute-start.17 = (bf16[32,3200]{1,0:T(8,128)(2,1)}, bf16[32,3200]{1,0:T(8,128)(2,1)S(1)}, u32[]{:S(2)}, u32[]{:S(2)}) collective-permute-start(bf16[32,3200]{1,0:T(8,128)(2,1)} %get-tuple-element.57), channel_id=1, source_target_pairs={{0,64},{1,17},{2,66},{3,19},{4,68},{5,21},{6,70},{7,23},{8,72},{9,... | collective-permute-start | bytes 614408 | tf_op jit(solution)/shard_map/ppermute | solution.py:58
  143.2 7.3 %collective-permute-start.18 = (bf16[32,3200]{1,0:T(8,128)(2,1)}, bf16[32,3200]{1,0:T(8,128)(2,1)S(1)}, u32[]{:S(2)}, u32[]{:S(2)}) collective-permute-start(bf16[32,3200]{1,0:T(8,128)(2,1)} %get-tuple-element.58), channel_id=1, source_target_pairs={{0,32},{1,9},{2,34},{3,11},{4,36},{5,13},{6,38},{7,15},{8,40},{9,1... | collective-permute-start | bytes 614408 | tf_op jit(solution)/shard_map/ppermute | solution.py:58
  156.3 7.3 %collective-permute-start.22 = (bf16[32,2048]{1,0:T(8,128)(2,1)}, bf16[32,2048]{1,0:T(8,128)(2,1)S(1)}, u32[]{:S(2)}, u32[]{:S(2)}) collective-permute-start(bf16[32,2048]{1,0:T(8,128)(2,1)} %get-tuple-element.62), channel_id=1, source_target_pairs={{0,32},{1,9},{2,34},{3,11},{4,36},{5,13},{6,38},{7,15},{8,40},{9,1... | collective-permute-start | bytes 393224 | tf_op jit(solution)/shard_map/ppermute | solution.py:58
  163.6 8.9 %collective-permute-start.25 = (bf16[128,2048]{1,0:T(8,128)(2,1)S(1)}, bf16[128,2048]{1,0:T(8,128)(2,1)S(1)}, u32[]{:S(2)}, u32[]{:S(2)}) collective-permute-start(bf16[128,2048]{1,0:T(8,128)(2,1)S(1)} %constant_dynamic-update-slice_fusion.4.a0), channel_id=1, source_target_pairs={{0,8},{1,33},{2,10},{3,35},{4,12},{5,37},{6,14},{7,39},{8,16},{9,4... | collective-permute-start | bytes 1572872 | tf_op jit(solution)/shard_map/ppermute | solution.py:58
  164.8 9.6 %collective-permute-start.24 = (bf16[128,2048]{1,0:T(8,128)(2,1)S(1)}, bf16[128,2048]{1,0:T(8,128)(2,1)S(1)}, u32[]{:S(2)}, u32[]{:S(2)}) collective-permute-start(bf16[128,2048]{1,0:T(8,128)(2,1)S(1)} %constant_dynamic-update-slice_fusion.4.a0), channel_id=1, source_target_pairs={{0,16},{1,65},{2,18},{3,67},{4,20},{5,69},{6,22},{7,71},{8,24},{9,... | collective-permute-start | bytes 1572872 | tf_op jit(solution)/shard_map/ppermute | solution.py:58
  167.4 12.8 %collective-permute-start.23 = (bf16[128,2048]{1,0:T(8,128)(2,1)S(1)}, bf16[128,2048]{1,0:T(8,128)(2,1)S(1)}, u32[]{:S(2)}, u32[]{:S(2)}) collective-permute-start(bf16[128,2048]{1,0:T(8,128)(2,1)S(1)} %constant_dynamic-update-slice_fusion.4.a0), channel_id=1, source_target_pairs={{0,24},{1,97},{2,26},{3,99},{4,28},{5,101},{6,30},{7,103},{8,0},{9... | collective-permute-start | bytes 1572872 | tf_op jit(solution)/shard_map/ppermute | solution.py:58
  194.9 9.4 %collective-permute-start.27 = (bf16[256,512]{1,0:T(8,128)(2,1)S(1)}, bf16[256,512]{1,0:T(8,128)(2,1)S(1)}, u32[]{:S(2)}, u32[]{:S(2)}) collective-permute-start(bf16[256,512]{1,0:T(8,128)(2,1)S(1)} %add_convert_fusion.1), channel_id=1, source_target_pairs={{0,2},{2,4},{4,6},{1,3},{3,5},{5,7},{8,10},{10,12},{12,14},{9,11},... | collective-permute-start | bytes 786440 | tf_op jit(solution)/shard_map/ppermute | solution.py:445
  214.9 13.3 %collective-permute-start.28 = (bf16[128,3200]{1,0:T(8,128)(2,1)}, bf16[128,3200]{1,0:T(8,128)(2,1)S(1)}, u32[]{:S(2)}, u32[]{:S(2)}) collective-permute-start(bf16[128,3200]{1,0:T(8,128)(2,1)} %get-tuple-element.66), channel_id=1, source_target_pairs={{0,16},{1,65},{2,18},{3,67},{4,20},{5,69},{6,22},{7,71},{8,24},{9,... | collective-permute-start | bytes 2457608 | tf_op jit(solution)/shard_map/ppermute | solution.py:58
  217.3 19.0 %collective-permute-start.29 = (bf16[128,3200]{1,0:T(8,128)(2,1)}, bf16[128,3200]{1,0:T(8,128)(2,1)S(1)}, u32[]{:S(2)}, u32[]{:S(2)}) collective-permute-start(bf16[128,3200]{1,0:T(8,128)(2,1)} %get-tuple-element.67), channel_id=1, source_target_pairs={{0,8},{1,33},{2,10},{3,35},{4,12},{5,37},{6,14},{7,39},{8,16},{9,4... | collective-permute-start | bytes 2457608 | tf_op jit(solution)/shard_map/ppermute | solution.py:58
  217.3 19.7 %collective-permute-start.30 = (bf16[128,3200]{1,0:T(8,128)(2,1)}, bf16[128,3200]{1,0:T(8,128)(2,1)S(1)}, u32[]{:S(2)}, u32[]{:S(2)}) collective-permute-start(bf16[128,3200]{1,0:T(8,128)(2,1)} %get-tuple-element.68), channel_id=1, source_target_pairs={{0,24},{1,97},{2,26},{3,99},{4,28},{5,101},{6,30},{7,103},{8,0},{9... | collective-permute-start | bytes 2457608 | tf_op jit(solution)/shard_map/ppermute | solution.py:58
  242.8 6.7 %collective-permute-start.31 = (bf16[32,3200]{1,0:T(8,128)(2,1)}, bf16[32,3200]{1,0:T(8,128)(2,1)S(1)}, u32[]{:S(2)}, u32[]{:S(2)}) collective-permute-start(bf16[32,3200]{1,0:T(8,128)(2,1)} %get-tuple-element.70), channel_id=1, source_target_pairs={{0,64},{1,17},{2,66},{3,19},{4,68},{5,21},{6,70},{7,23},{8,72},{9,... | collective-permute-start | bytes 614408 | tf_op jit(solution)/shard_map/ppermute | solution.py:58
  244.5 7.2 %collective-permute-start.32 = (bf16[32,3200]{1,0:T(8,128)(2,1)}, bf16[32,3200]{1,0:T(8,128)(2,1)S(1)}, u32[]{:S(2)}, u32[]{:S(2)}) collective-permute-start(bf16[32,3200]{1,0:T(8,128)(2,1)} %get-tuple-element.71), channel_id=1, source_target_pairs={{0,32},{1,9},{2,34},{3,11},{4,36},{5,13},{6,38},{7,15},{8,40},{9,1... | collective-permute-start | bytes 614408 | tf_op jit(solution)/shard_map/ppermute | solution.py:58
  323.6 103.6 %all-to-all-start = ((bf16[64,32,2,512]{3,2,1,0:T(2,128)(2,1)}), bf16[64,32,2,512]{3,2,1,0:T(2,128)(2,1)}, u32[]{:S(2)}, u32[]{:S(2)}) async-start(bf16[64,32,2,512]{3,2,1,0:T(2,128)(2,1)} %ship.1), calls=%async_computation | async-start | bytes 8388608 | tf_op jit(solution)/shard_map/all_to_all | solution.py:497
  345.2 54.6 %collective-permute-start.36 = (bf16[32,2048]{1,0:T(8,128)(2,1)S(1)}, bf16[32,2048]{1,0:T(8,128)(2,1)S(1)}, u32[]{:S(2)}, u32[]{:S(2)}) collective-permute-start(bf16[32,2048]{1,0:T(8,128)(2,1)S(1)} %copy-done.35), channel_id=1, source_target_pairs={{0,32},{1,9},{2,34},{3,11},{4,36},{5,13},{6,38},{7,15},{8,40},{9,1... | collective-permute-start | bytes 393224 | tf_op jit(solution)/shard_map/ppermute | solution.py:58
  346.2 53.6 %collective-permute-start.35 = (bf16[32,2048]{1,0:T(8,128)(2,1)S(1)}, bf16[32,2048]{1,0:T(8,128)(2,1)S(1)}, u32[]{:S(2)}, u32[]{:S(2)}) collective-permute-start(bf16[32,2048]{1,0:T(8,128)(2,1)S(1)} %copy-done.35), channel_id=1, source_target_pairs={{0,64},{1,17},{2,66},{3,19},{4,68},{5,21},{6,70},{7,23},{8,72},{9,... | collective-permute-start | bytes 393224 | tf_op jit(solution)/shard_map/ppermute | solution.py:58
  346.7 53.1 %collective-permute-start.34 = (bf16[32,2048]{1,0:T(8,128)(2,1)S(1)}, bf16[32,2048]{1,0:T(8,128)(2,1)S(1)}, u32[]{:S(2)}, u32[]{:S(2)}) collective-permute-start(bf16[32,2048]{1,0:T(8,128)(2,1)S(1)} %copy-done.35), channel_id=1, source_target_pairs={{0,96},{1,25},{2,98},{3,27},{4,100},{5,29},{6,102},{7,31},{8,104},... | collective-permute-start | bytes 393224 | tf_op jit(solution)/shard_map/ppermute | solution.py:58
  399.9 8.4 %collective-permute-start.39 = (bf16[128,2048]{1,0:T(8,128)(2,1)S(1)}, bf16[128,2048]{1,0:T(8,128)(2,1)S(1)}, u32[]{:S(2)}, u32[]{:S(2)}) collective-permute-start(bf16[128,2048]{1,0:T(8,128)(2,1)S(1)} %constant_dynamic-update-slice_fusion.8.a0), channel_id=1, source_target_pairs={{0,8},{1,33},{2,10},{3,35},{4,12},{5,37},{6,14},{7,39},{8,16},{9,4... | collective-permute-start | bytes 1572872 | tf_op jit(solution)/shard_map/ppermute | solution.py:58
  400.7 9.9 %collective-permute-start.38 = (bf16[128,2048]{1,0:T(8,128)(2,1)S(1)}, bf16[128,2048]{1,0:T(8,128)(2,1)S(1)}, u32[]{:S(2)}, u32[]{:S(2)}) collective-permute-start(bf16[128,2048]{1,0:T(8,128)(2,1)S(1)} %constant_dynamic-update-slice_fusion.8.a0), channel_id=1, source_target_pairs={{0,16},{1,65},{2,18},{3,67},{4,20},{5,69},{6,22},{7,71},{8,24},{9,... | collective-permute-start | bytes 1572872 | tf_op jit(solution)/shard_map/ppermute | solution.py:58
  402.8 13.1 %collective-permute-start.37 = (bf16[128,2048]{1,0:T(8,128)(2,1)S(1)}, bf16[128,2048]{1,0:T(8,128)(2,1)S(1)}, u32[]{:S(2)}, u32[]{:S(2)}) collective-permute-start(bf16[128,2048]{1,0:T(8,128)(2,1)S(1)} %constant_dynamic-update-slice_fusion.8.a0), channel_id=1, source_target_pairs={{0,24},{1,97},{2,26},{3,99},{4,28},{5,101},{6,30},{7,103},{8,0},{9... | collective-permute-start | bytes 1572872 | tf_op jit(solution)/shard_map/ppermute | solution.py:58
  (51 other events, 431.7 us)
